TPU v7x, 32 devices: a whole 2x2x4 slice. The times are simulated.
32 devices in a mesh: dp: 4 (over x, core), mem: 8 (over z, y).
Axes of the slice: x: 2, y: 2, z: 4, core: 2. Of those that a mesh axis runs over, the one named last changes fastest.
Arguments:
- tokens: bfloat16 [16384, 2048], P(('dp', 'mem')), may hold values from -6 to 6
- span_bounds: int32 [2, 1024], P(None, ('dp', 'mem')), may hold values from 0 to 512, as said below
- mention_entity: int32 [1024], P(('dp', 'mem')), may hold values from 0 to 1023, as said below
- entity_cluster: int32 [1024], P('mem'), may hold values from 0 to 63, as said below
- entity_table: bfloat16 [1024, 2048], P('mem'), may hold values from -16 to 16
- w_out: bfloat16 [2048, 2048], replicated, may hold values from -0.125 to 0.125
Outputs:
- memory_out: bfloat16 [16384, 2048], P(('dp', 'mem'))
Inputs may be any that keep to these rules, and one draw needn't show every extreme that they name: `span_bounds`: mention i lies in segment i // 32; row 0 holds its start and row 1 its exclusive end, counted from the segment's first token, with start < end. `mention_entity`: entity e belongs to memory shard e // 128. Among the 32 mentions of each device, those naming entities of one shard number exactly 4, and those of every other shard number (28) // 7 or one more. `entity_cluster`: each cluster holds exactly 16 entities.
All inputs are finite; a program needn't handle non-finite values.
Results may differ from a plain program's by a relative error of at most 0.017.
Values may be sent and summed in bfloat16 or wider, within the bound.
A program may use at most 320 MiB of HBM per device.

v0:
```python
import math

import jax
import jax.numpy as jnp
from jax import lax
from jax.sharding import PartitionSpec as P

HEADS = 32
HEAD_DIM = 64
SEG = 512
MENT_SEG = 32
CL_SIZE = 16


def rms_rows(values):
    return values * lax.rsqrt(jnp.mean(values * values, axis=-1, keepdims=True) + 1e-06)


def on_device(tokens, span_bounds, mention_entity, entity_cluster, entity_table, w_out):
    model_width = tokens.shape[1]
    ent_rows = entity_table.shape[0]
    shards = lax.axis_size("mem")
    segments = tokens.shape[0] // SEG
    scale = HEAD_DIM ** (-0.5)
    seg_tokens = tokens.reshape(segments, SEG, model_width)
    starts = span_bounds[0].reshape(segments, MENT_SEG)
    ends = span_bounds[1].reshape(segments, MENT_SEG)
    positions = jnp.arange(SEG, dtype=jnp.int32)
    covered = (
        (positions[None, None, :] >= starts[:, :, None])
        & (positions[None, None, :] < ends[:, :, None])
    ).astype(jnp.bfloat16)
    span_sums = jnp.einsum("smp,spd->smd", covered, seg_tokens, preferred_element_type=jnp.float32)
    span_len = (ends - starts).astype(jnp.float32)
    mention_vec = (span_sums / span_len[:, :, None]).reshape(-1, model_width).astype(jnp.bfloat16)
    wanted = jnp.arange(ent_rows * lax.axis_size("mem"), dtype=jnp.int32)
    picking = (wanted[:, None] == mention_entity[None, :]).astype(jnp.bfloat16)
    pooled = lax.psum_scatter(
        jnp.dot(picking, mention_vec, preferred_element_type=jnp.float32).astype(jnp.bfloat16),
        "mem",
        scatter_dimension=0,
        tiled=True,
    ).astype(jnp.float32)
    pooled = lax.psum(pooled.astype(jnp.bfloat16), "dp").astype(jnp.float32)
    entity_state = rms_rows(entity_table.astype(jnp.float32) + pooled).astype(jnp.bfloat16)
    cluster_count = ent_rows * shards // CL_SIZE
    grouping = (
        jnp.arange(cluster_count, dtype=jnp.int32)[:, None] == entity_cluster[None, :]
    ).astype(jnp.bfloat16)
    partial_groups = jnp.dot(grouping, entity_state, preferred_element_type=jnp.float32)
    cluster_state = rms_rows(
        lax.psum(partial_groups.astype(jnp.bfloat16), "mem").astype(jnp.float32)
    ).astype(jnp.bfloat16)
    queries = tokens.reshape(segments, SEG, HEADS, HEAD_DIM)
    cluster_heads = cluster_state.reshape(-1, HEADS, HEAD_DIM)

    def cluster_read(segment_queries):
        scores = (
            jnp.einsum(
                "thd,khd->htk", segment_queries, cluster_heads, preferred_element_type=jnp.float32
            )
            * scale
        )
        probs = jnp.exp(scores - jnp.max(scores, axis=-1, keepdims=True))
        totals = jnp.sum(probs, axis=-1)
        weighted = jnp.einsum(
            "htk,khd->thd",
            probs.astype(jnp.bfloat16),
            cluster_heads,
            preferred_element_type=jnp.float32,
        )
        return weighted / jnp.transpose(totals)[:, :, None]

    cluster_part = lax.map(cluster_read, queries)
    start_state = (
        jnp.full((segments, HEADS, SEG), -1e30, jnp.float32),
        jnp.zeros((segments, HEADS, SEG), jnp.float32),
        jnp.zeros((segments, SEG, HEADS, HEAD_DIM), jnp.float32),
    )
    running = start_state
    piece_heads = lax.all_gather(entity_state, "mem", axis=0, tiled=True).reshape(
        -1, HEADS, HEAD_DIM
    )
    piece_rows = piece_heads.shape[0]
    block_rows = math.gcd(piece_rows, 512)
    for block_start in range(0, piece_rows, block_rows):
        key_rows = piece_heads[block_start : block_start + block_rows]

        def update(packed):
            segment_queries, row_max, totals, weighted = packed
            scores = (
                jnp.einsum(
                    "thd,khd->htk", segment_queries, key_rows, preferred_element_type=jnp.float32
                )
                * scale
            )
            new_max = jnp.maximum(row_max, jnp.max(scores, axis=-1))
            rescale = jnp.exp(row_max - new_max)
            probs = jnp.exp(scores - new_max[:, :, None])
            totals = totals * rescale + jnp.sum(probs, axis=-1)
            added = jnp.einsum(
                "htk,khd->thd",
                probs.astype(jnp.bfloat16),
                key_rows,
                preferred_element_type=jnp.float32,
            )
            weighted = weighted * jnp.transpose(rescale)[:, :, None] + added
            return (new_max, totals, weighted)

        running = lax.map(update, (queries, running[0], running[1], running[2]))
    row_max, totals, weighted = running
    entity_part = weighted / jnp.transpose(totals, (0, 2, 1))[:, :, :, None]
    readout = (entity_part + cluster_part).astype(jnp.bfloat16).reshape(-1, model_width)
    projected = jnp.dot(readout, w_out, preferred_element_type=jnp.float32)
    return rms_rows(projected).astype(jnp.bfloat16)


def solution(mesh):
    placed = (
        P(("dp", "mem"), None),
        P(None, ("dp", "mem")),
        P(("dp", "mem")),
        P("mem"),
        P("mem", None),
        P(),
    )
    return jax.shard_map(
        on_device, mesh=mesh, in_specs=placed, out_specs=P(("dp", "mem"), None), check_vma=False
    )
```

profile of v0, /device:TPU:0, one launch (start us, length us, event | category | flops | bytes accessed | tf_op | source)
XLA Modules:
  0.0 403.3 jit_solution(9410979848685327895)
XLA Ops:
  6.5 0.0 reduce-scatter.2.cloned.1.call-start
  6.5 0.8 slice_bitcast_fusion.1
  7.3 0.0 copy-start.2
  7.3 5.2 %convolution_convert_fusion = bf16[1024,2048]{1,0:T(8,128)(2,1)} fusion(bf16[512,2048]{1,0:T(8,128)(2,1)} %param.6, s32[32]{0:T(128)} %param.8, f32[32]{0:T(128)S(1)} %get-tuple-element.56, s32[32]{0:T(128)S(1)} %get-tuple-element.57, s32[32]{0:T(128)S(1)} %get-tuple-element.47), kind=kOutput, calls=%fused_computation.28 | convolution fusion | flops 203636736 | bytes 6291968 | tf_op jit(solution)/shard_map/dot_general | solution.py:39
  12.5 0.0 copy-start.3
  12.5 0.0 reduce-scatter.2.cloned.1.call-update
  12.5 0.0 all-reduce.3.cloned.1.call-start
  12.6 90.9 %reduce-scatter.2.cloned.1.call-done = bf16[128,2048]{1,0:T(8,128)(2,1)} async-done(((bf16[1024,2048]{1,0:T(8,128)(2,1)}), bf16[128,2048]{1,0:T(8,128)(2,1)}) %reduce-scatter.2.cloned.1.call-update) | async-done | bytes 524304 | tf_op jit(solution)/shard_map/reduce_scatter | solution.py:38
  103.4 0.0 all-reduce.3.cloned.1.call-update
  103.5 0.0 all-reduce.5.cloned.1.call-start
  103.5 35.4 %all-reduce.3.cloned.1.call-done = bf16[128,2048]{1,0:T(8,128)(2,1)} async-done(((bf16[128,2048]{1,0:T(8,128)(2,1)}), bf16[128,2048]{1,0:T(8,128)(2,1)}) %all-reduce.3.cloned.1.call-update) | async-done | bytes 524304 | tf_op jit(solution)/shard_map/psum | solution.py:44
  138.9 0.0 copy-done.2
  138.9 1.3 multiply_reduce_fusion.1
  140.2 1.2 multiply_convert_fusion.1
  141.4 0.0 copy-start.1
  141.4 0.0 copy-done.3
  141.4 0.9 convolution_convert_fusion.1
  142.3 0.0 all-reduce.5.cloned.1.call-update
  142.4 0.2 all-gather.2.cloned.1.call-start
  142.6 0.0 copy-done.1
  142.6 0.3 all-gather.2.cloned.1.call-update
  142.9 2.9 copy.19
  145.8 67.4 %all-reduce.5.cloned.1.call-done = bf16[64,2048]{1,0:T(8,128)(2,1)} async-done(((bf16[64,2048]{1,0:T(8,128)(2,1)}), bf16[64,2048]{1,0:T(8,128)(2,1)}) %all-reduce.5.cloned.1.call-update) | async-done | bytes 262160 | tf_op jit(solution)/shard_map/psum | solution.py:52
  213.2 1.1 fusion.28
  214.3 1.1 fusion.29
  215.4 0.3 copy.27
  215.7 0.8 bitcast_reduce_fusion.2
  216.4 0.9 fusion.19
  217.3 2.8 fusion.24
  220.1 67.8 %all-gather.2.cloned.1.call-done = bf16[1024,2048]{1,0:T(8,128)(2,1)} async-done(((bf16[128,2048]{1,0:T(8,128)(2,1)}), bf16[1024,2048]{1,0:T(8,128)(2,1)}) %all-gather.2.cloned.1.call-update) | async-done | bytes 4194320 | tf_op jit(solution)/shard_map/all_gather | solution.py:81
  287.9 4.8 %fusion.53 = (bf16[512,2048]{1,0:T(8,128)(2,1)}, bf16[512,2048]{1,0:T(8,128)(2,1)}) fusion(bf16[1024,2048]{1,0:T(8,128)(2,1)} %all-gather.2.cloned.1.call-done), kind=kLoop, calls=%fused_computation.79 | loop fusion | bytes 8388608 | tf_op jit(solution)/shard_map/slice | solution.py:87
  292.8 3.9 copy.18
  296.7 14.9 %bitcast_reduce_fusion.1 = (f32[32,512]{1,0:T(8,128)S(1)}, f32[32,512,512]{2,1,0:T(8,128)}) fusion(bf16[512,32,64]{0,2,1:T(8,128)(2,1)} %bitcast.110, bf16[512,32,64]{0,2,1:T(8,128)(2,1)S(1)} %bitcast.106), kind=kOutput, calls=%fused_computation.4 | convolution fusion | flops 1090502656 | bytes 37814272 | tf_op jit(solution)/shard_map/while/body/eval_jaxpr/thd,khd->htk/dot_general | solution.py:92
  311.6 3.9 copy.21
  315.5 14.8 %bitcast_reduce_fusion = (f32[32,512]{1,0:T(8,128)S(1)}, f32[32,512,512]{2,1,0:T(8,128)}) fusion(bf16[512,32,64]{0,2,1:T(8,128)(2,1)} %bitcast.108, bf16[512,32,64]{0,2,1:T(8,128)(2,1)S(1)} %bitcast.107), kind=kOutput, calls=%fused_computation.1 | convolution fusion | flops 1090502656 | bytes 37814272 | tf_op jit(solution)/shard_map/while/body/eval_jaxpr/thd,khd->htk/dot_general | solution.py:92
  330.4 16.3 %fusion.6 = f32[32,64,512]{2,1,0:T(8,128)} fusion(bf16[512,32,64]{0,2,1:T(8,128)(2,1)} %bitcast.109, f32[32,512,512]{2,1,0:T(8,128)} %get-tuple-element.63, f32[32,512]{1,0:T(8,128)S(1)} %get-tuple-element.46), kind=kOutput, calls=%fused_computation.10 | convolution fusion | flops 1098907648 | bytes 39911424 | tf_op jit(solution)/shard_map/while/body/eval_jaxpr/htk,khd->thd/dot_general | solution.py:101
  346.7 0.0 copy-start
  346.7 22.8 %fusion.2 = (f32[32,512]{1,0:T(8,128)S(1)}, f32[32,512]{1,0:T(8,128)S(1)}) fusion(f32[32,512,512]{2,1,0:T(8,128)} %get-tuple-element.61, f32[32,512]{1,0:T(8,128)S(1)} %get-tuple-element.45, f32[32,512]{1,0:T(8,128)S(1)} %get-tuple-element.46, f32[32,512,512]{2,1,0:T(8,128)} %get-tuple-element.63), kind=kLoop, calls=%fused_computation.6 | loop fusion | flops 50298880 | bytes 67371008 | tf_op jit(solution)/shard_map/while/body/eval_jaxpr/reduce_sum | solution.py:100
  369.6 0.0 copy-done
  369.6 17.8 %fusion.15 = bf16[512,32,64]{0,2,1:T(8,128)(2,1)} fusion(f32[32,64,512]{2,1,0:T(8,128)} %fusion.24, f32[32,64,512]{2,1,0:T(8,128)} %fusion.6, bf16[512,32,64]{0,2,1:T(8,128)(2,1)S(1)} %bitcast.111, f32[32,512,512]{2,1,0:T(8,128)} %get-tuple-element.61, f32[32,512]{1,0:T(8,128)S(1)} %get-tuple-element.45, f32[512,32]{0,1:T(8,128)S(1)} %bitcast.114, ...), kind=kOutput, calls=%fused_computation.18 | convolution fusion | flops 1106247680 | bytes 46465024 | tf_op jit(solution)/shard_map/while/body/eval_jaxpr/htk,khd->thd/dot_general | solution.py:101
  387.4 7.8 %multiply_reduce_fusion = (f32[512]{0:T(512)S(1)}, f32[512,2048]{1,0:T(8,128)S(1)}) fusion(bf16[512,2048]{0,1:T(8,128)(2,1)} %bitcast.115, bf16[2048,2048]{1,0:T(8,128)(2,1)} %param.11), kind=kOutput, calls=%fused_computation.27 | convolution fusion | flops 4297063936 | bytes 14682112 | tf_op jit(solution)/shard_map/dot_general | solution.py:114
  395.1 1.6 multiply_convert_fusion
  (6 shorter events, 0.1 us)
Async XLA Ops:
  6.5 96.9 %reduce-scatter.2.cloned.1.call-start = ((), (), s32[]{:S(2)}) async-start(), calls=%async_computation.1 | async-start | bytes 4718592 | tf_op jit(solution)/shard_map/reduce_scatter | solution.py:38
  7.3 131.6 %copy-start.2 = (bf16[128,2048]{1,0:T(8,128)(2,1)S(1)}, bf16[128,2048]{1,0:T(8,128)(2,1)}, u32[]{:S(2)}) copy-start(bf16[128,2048]{1,0:T(8,128)(2,1)} %param.10) | copy-start | bytes 1572868
  12.5 128.9 %copy-start.3 = (s32[128]{0:T(128)S(1)}, s32[128]{0:T(128)}, u32[]{:S(2)}) copy-start(s32[128]{0:T(128)} %param.9) | copy-start | bytes 1540
  12.5 126.3 %all-reduce.3.cloned.1.call-start = ((), (), s32[]{:S(2)}) async-start(), calls=%async_computation.2 | async-start | bytes 1048576 | tf_op jit(solution)/shard_map/psum | solution.py:44
  103.5 109.7 %all-reduce.5.cloned.1.call-start = ((), (), s32[]{:S(2)}) async-start(), calls=%async_computation.4 | async-start | bytes 524288 | tf_op jit(solution)/shard_map/psum | solution.py:52
  141.4 1.2 copy-start.1
  142.4 145.5 %all-gather.2.cloned.1.call-start = ((), (), s32[]{:S(2)}) async-start(), calls=%async_computation.3 | async-start | bytes 4718592 | tf_op jit(solution)/shard_map/all_gather | solution.py:81
  346.7 22.8 %copy-start = (bf16[512,2048]{0,1:T(8,128)(2,1)S(1)}, bf16[512,2048]{0,1:T(8,128)(2,1)}, u32[]{:S(2)}) copy-start(bf16[512,2048]{0,1:T(8,128)(2,1)} %copy.18) | copy-start | bytes 6291460
Sparse Core Ops, SparseCore 0:
  12.6 90.7 reduce-scatter.1
  105.9 32.9 all-reduce.2
  142.6 70.5 all-reduce.4
  215.2 72.6 all-gather.1
where the time goes:
time: 404 us; the launch traced here: 403 us
  waiting for transfers between devices  262 us (65%)
  matrix products  81.3 us (20%)
  other arithmetic  30.8 us (8%)
  local copies, waits for them, and re-layouts  15.8 us (4%)
  between operations  13.2 us (3%)
    reduce_scatter x1, waiting for transfers between devices, on_device(): lax.psum_scatter(jnp.dot(picking, mention_vec, preferred_element_type=jnp...  90.9 us
    all_gather x1, waiting for transfers between devices, on_device(): lax.all_gather(entity_state, 'mem', axis=0, tiled=True)  67.8 us
    psum x1, waiting for transfers between devices, on_device(): lax.psum(partial_groups.astype(jnp.bfloat16), 'mem').astype(jnp.float32)  67.4 us
    psum x1, waiting for transfers between devices, on_device(): pooled = lax.psum(pooled.astype(jnp.bfloat16), 'dp').astype(jnp.float32)  35.4 us
    dot_general x2, matrix products, update(): jnp.einsum('htk,khd->thd', probs.astype(jnp.bfloat16), key_rows, preferre...  34.1 us
    dot_general x2, matrix products, update(): jnp.einsum('thd,khd->htk', segment_queries, key_rows, preferred_element_t...  29.7 us
    reduce_sum x1, other arithmetic, update(): totals = totals * rescale + jnp.sum(probs, axis=-1)  22.8 us
    slice x3, local copies, waits for them, and re-layouts, on_device(): key_rows = piece_heads[block_start:block_start + block_rows]  12.7 us
  transfers between devices with their start and end apart: 4, of which 4 were waited for; matrix products, arithmetic and copies ran while one was open for 2% of the time, Pallas kernels for 0%

commit v1 on v0

v1 whole, which is shorter than its diff:
```python
import functools

import jax
import jax.numpy as jnp
from jax import lax
from jax.experimental import pallas as pl
from jax.experimental.pallas import tpu as pltpu
from jax.sharding import PartitionSpec as P

MESH = pl.DeviceIdType.MESH
HEAD_DIM = 64
CL_SIZE = 16
SLOTS = 4
PIECES = 4
BF16 = jnp.bfloat16
F32 = jnp.float32


def rms_rows(values):
    return values * lax.rsqrt(jnp.mean(values * values, axis=-1, keepdims=True) + 1e-06)


def ring_place(index, depth, width):
    z, y = index // width, index % width
    back = depth - 1 - z
    across = jnp.where(back % 2 == 0, y - 1, width - 1 - y)
    return jnp.where(y == 0, z, depth + back * (width - 1) + across)


def ring_device(place, depth, width):
    rest = jnp.maximum(place - depth, 0)
    back, across = rest // (width - 1), rest % (width - 1)
    y = jnp.where(back % 2 == 0, 1 + across, width - 1 - across)
    return jnp.where(place < depth, place * width, (depth - 1 - back) * width + y)


def exchange_kernel(
    n, groups, tokens, bounds, ent_col, ent_row, cluster_col, table,
    states_out, cluster_out,
    outbox, mentions, states, pooled,
    mem_send, mem_recv, dp_send, dp_recv, pair_send, pair_recv, own_sem,
    ring_send, ring_recv, hand_send, hand_recv, out_sem,
):
    d = table.shape[1]
    rows = table.shape[0]
    piece = d // PIECES
    depth, width = 4, n // 4
    me, row = lax.axis_index("mem"), lax.axis_index("dp")
    core = row % 2
    sibling = row + 1 - 2 * core
    place = ring_place(me, depth, width)
    right = ring_device((place + 1) % n, depth, width)
    left = ring_device((place + n - 1) % n, depth, width)
    xs = groups // 2

    barrier = pltpu.get_barrier_semaphore()
    for step in range(1, n):
        pl.semaphore_signal(barrier, device_id=(row, (me + step) % n), device_id_type=MESH)
    for step in range(1, xs):
        pl.semaphore_signal(barrier, device_id=((row + 2 * step) % groups, me), device_id_type=MESH)
    pl.semaphore_signal(barrier, device_id=(sibling, me), device_id_type=MESH)

    count = bounds.shape[0]
    position = lax.broadcasted_iota(jnp.int32, (count, tokens.shape[0]), 1)
    covered = (position >= bounds[:, 0:1]) & (position < bounds[:, 1:2])
    sums = jnp.dot(covered.astype(F32).astype(BF16), tokens[...], preferred_element_type=F32)
    vectors = (sums / (bounds[:, 1:2] - bounds[:, 0:1]).astype(F32)).astype(BF16)
    shard_col, shard_row = ent_col[...] // rows, ent_row[...] // rows
    first = lax.broadcasted_iota(jnp.int32, (count, count), 0)
    second = lax.broadcasted_iota(jnp.int32, (count, count), 1)
    rank = jnp.sum(((shard_col == shard_row) & (first < second)).astype(jnp.int32), axis=0, keepdims=True)
    slot_row = shard_row * SLOTS + rank
    total = n * SLOTS * PIECES
    line = lax.broadcasted_iota(jnp.int32, (total, count), 0)
    match = slot_row == (line // (SLOTS * PIECES)) * SLOTS + line % SLOTS
    part = (line // SLOTS) % PIECES
    packed = jnp.zeros((total, piece), F32)
    for p in range(PIECES):
        pick = (match & (part == p)).astype(F32).astype(BF16)
        packed += jnp.dot(pick, vectors[:, p * piece:(p + 1) * piece], preferred_element_type=F32)
    local = (ent_row[...] - shard_row * rows + 1).astype(F32)
    ids = jnp.sum(jnp.where(match, local, 0.0), axis=1, keepdims=True) - 1.0
    outbox[:, :, :piece] = packed.astype(BF16).reshape(n, SLOTS * PIECES, piece)
    outbox[:, :, piece:] = jnp.broadcast_to(ids, (total, 128)).astype(BF16).reshape(n, SLOTS * PIECES, 128)

    pl.semaphore_wait(barrier, n - 1 + xs)

    own = pltpu.make_async_copy(outbox.at[me], mentions.at[row, me], own_sem)
    own.start()
    sends = []
    for step in range(1, n):
        to = (me + step) % n
        copy = pltpu.make_async_remote_copy(
            outbox.at[to], mentions.at[row, me], mem_send.at[step], mem_recv.at[step],
            device_id=(row, to), device_id_type=MESH)
        copy.start()
        sends.append(copy)
    own.wait()
    for step in range(1, n):
        src = (me + n - step) % n
        pltpu.make_async_remote_copy(
            outbox.at[src], mentions.at[row, src], mem_send.at[step], mem_recv.at[step],
            device_id=(row, src), device_id_type=MESH).wait_recv()

    def to_replica(block, to, send, recv):
        return pltpu.make_async_remote_copy(
            mentions.at[block], mentions.at[block], send, recv, device_id=(to, me), device_id_type=MESH)

    for step in range(1, xs):
        copy = to_replica(row, (row + 2 * step) % groups, dp_send.at[step], dp_recv.at[step])
        copy.start()
        sends.append(copy)
    copy = to_replica(row, sibling, pair_send.at[0], pair_recv.at[0])
    copy.start()
    sends.append(copy)
    for step in range(1, xs):
        src = (row + groups - 2 * step) % groups
        to_replica(src, src, dp_send.at[step], dp_recv.at[step]).wait_recv()
        copy = to_replica(src, sibling, pair_send.at[step], pair_recv.at[step])
        copy.start()
        sends.append(copy)
    for step in range(xs):
        src = (sibling + groups - 2 * step) % groups
        to_replica(src, sibling, pair_send.at[step], pair_recv.at[step]).wait_recv()

    arrived = groups * n * SLOTS * PIECES
    box = mentions[...].reshape(arrived, piece + 128)
    line = lax.broadcasted_iota(jnp.int32, (arrived, rows), 0)
    entity = lax.broadcasted_iota(jnp.int32, (arrived, rows), 1).astype(F32)
    named = box[:, piece:].astype(F32) == entity
    part = (line // SLOTS) % PIECES
    square = jnp.zeros((rows, 1), F32)
    for p in range(PIECES):
        pick = (named & (part == p)).astype(F32).astype(BF16)
        got = lax.dot_general(pick, box[:, :piece], (((0,), (0,)), ((), ())), preferred_element_type=F32)
        got += table[:, p * piece:(p + 1) * piece].astype(F32)
        pooled[:, p * piece:(p + 1) * piece] = got
        square += jnp.sum(got * got, axis=-1, keepdims=True)
    state = (pooled[...] * lax.rsqrt(square / d + 1e-06)).astype(BF16)
    quarter = rows // 4
    states[0, :, :, :d] = state.reshape(4, quarter, d)
    kind = lax.broadcasted_iota(jnp.int32, (rows, 128), 1)
    group = (cluster_col[...] == kind).astype(F32).astype(BF16)
    states[0, :, :, d:] = group.reshape(4, quarter, 128)

    half = n // 2

    def portion(way, step):
        if step < half:
            return pl.ds(2 * core, 2)
        return pl.ds(2 * core + way, 1)

    def ring_copy(way, step):
        src = step - 1 if way == 0 else (n - step + 1) % n
        dst = step if way == 0 else n - step
        quarters = portion(way, step)
        return pltpu.make_async_remote_copy(
            states.at[src, quarters], states.at[dst, quarters], ring_send.at[way, step], ring_recv.at[way, step],
            device_id=(row, right if way == 0 else left), device_id_type=MESH)

    def hand_copy(way, step, to_core):
        dst = step if way == 0 else n - step
        if step < half:
            quarters = pl.ds(2 * to_core, 2)
        else:
            quarters = pl.ds(2 * to_core + way, 1)
        return pltpu.make_async_remote_copy(
            states.at[dst, quarters], states.at[dst, quarters], hand_send.at[way, step], hand_recv.at[way, step],
            device_id=(sibling, me), device_id_type=MESH)

    def out_copy(slot):
        return pltpu.make_async_copy(
            states.at[slot, :, :, pl.ds(0, d)], states_out.at[slot], out_sem.at[slot])

    outs = [out_copy(0)]
    outs[0].start()
    for step in range(1, half + 1):
        for way in range(2):
            if step > 1:
                ring_copy(way, step - 1).wait_recv()
            copy = ring_copy(way, step)
            copy.start()
            sends.append(copy)
            if step > 1:
                copy = hand_copy(way, step - 1, core)
                copy.start()
                sends.append(copy)
    for way in range(2):
        ring_copy(way, half).wait_recv()
        copy = hand_copy(way, half, core)
        copy.start()
        sends.append(copy)
    for step in range(1, half + 1):
        for way in range(2):
            hand_copy(way, step, 1 - core).wait_recv()
            if step < half:
                slot = step if way == 0 else n - step
                outs.append(out_copy(slot))
                outs[-1].start()
    outs.append(out_copy(half))
    outs[-1].start()

    clusters = cluster_out.shape[0]
    every = states[...].reshape(n * rows, d + 128)
    grouped = lax.dot_general(every[:, d:], every[:, :d], (((0,), (0,)), ((), ())), preferred_element_type=F32)
    cluster_out[...] = rms_rows(grouped[:clusters]).astype(BF16)
    for copy in outs:
        copy.wait()
    for copy in sends:
        copy.wait_send()


def exchange(n, groups, tokens, span_bounds, mention_entity, entity_cluster, table):
    rows, d = table.shape
    count = mention_entity.shape[0]
    clusters = rows * n // CL_SIZE
    piece = d // PIECES
    vmem = pl.BlockSpec(memory_space=pltpu.VMEM)
    dma = pltpu.SemaphoreType.DMA
    return pl.pallas_call(
        functools.partial(exchange_kernel, n, groups),
        out_shape=(jax.ShapeDtypeStruct((n, 4, rows // 4, d), BF16), jax.ShapeDtypeStruct((clusters, d), BF16)),
        in_specs=[vmem] * 6,
        out_specs=(pl.BlockSpec(memory_space=pl.ANY), vmem),
        scratch_shapes=[
            pltpu.VMEM((n, SLOTS * PIECES, piece + 128), BF16),
            pltpu.VMEM((groups, n, SLOTS * PIECES, piece + 128), BF16),
            pltpu.VMEM((n, 4, rows // 4, d + 128), BF16),
            pltpu.VMEM((rows, d), F32),
            dma((n,)), dma((n,)), dma((groups,)), dma((groups,)), dma((groups,)), dma((groups,)), dma,
            dma((2, n)), dma((2, n)), dma((2, n)), dma((2, n)), dma((n,)),
        ],
        compiler_params=pltpu.CompilerParams(
            collective_id=0, has_side_effects=True, vmem_limit_bytes=48 * 2**20),
    )(tokens, span_bounds.T, mention_entity.reshape(count, 1), mention_entity.reshape(1, count),
      entity_cluster.reshape(rows, 1), table)


def read_kernel(q_ref, k_ref, c_ref, w_hbm, out_ref, readout, weights, sem):
    g = pl.program_id(0)
    width = q_ref.shape[1]
    load = pltpu.make_async_copy(w_hbm, weights, sem)

    @pl.when(g == 0)
    def _():
        load.start()

    low = lax.broadcasted_iota(jnp.int32, (1, width), 1) < HEAD_DIM
    one, zero = jnp.ones((), BF16), jnp.zeros((), BF16)
    q = q_ref[...] * BF16(HEAD_DIM ** -0.5)
    queries = (jnp.where(low, q, zero), jnp.where(low, zero, q))
    total = None
    for ref in (k_ref, c_ref):
        keys = ref[...]
        values = (jnp.where(low, keys, one), jnp.where(low, one, keys))
        sides = []
        for h in range(2):
            scores = lax.dot_general(
                queries[h], keys, (((1,), (1,)), ((), ())), preferred_element_type=F32)
            probs = jnp.exp(scores - jnp.max(scores, axis=-1, keepdims=True)).astype(BF16)
            sides.append(jnp.dot(probs, values[h], preferred_element_type=F32))
        read = jnp.where(low, sides[0], sides[1]) / pltpu.roll(
            jnp.where(low, sides[1], sides[0]), HEAD_DIM, 1)
        total = read if total is None else total + read
    readout[:, pl.ds(pl.multiple_of(g * width, width), width)] = total.astype(BF16)

    @pl.when(g == pl.num_programs(0) - 1)
    def _():
        load.wait()
        projected = jnp.dot(readout[...], weights[...], preferred_element_type=F32)
        out_ref[...] = rms_rows(projected).astype(BF16)


def read_memories(queries, keys, clusters, w_out):
    tokens, d = queries.shape
    width = 2 * HEAD_DIM
    columns = lambda g: (0, g)
    return pl.pallas_call(
        read_kernel,
        grid=(d // width,),
        in_specs=[
            pl.BlockSpec((tokens, width), columns),
            pl.BlockSpec((keys.shape[0], width), columns),
            pl.BlockSpec((clusters.shape[0], width), columns),
            pl.BlockSpec(memory_space=pl.ANY),
        ],
        out_specs=pl.BlockSpec((tokens, d), lambda g: (0, 0)),
        out_shape=jax.ShapeDtypeStruct((tokens, d), BF16),
        scratch_shapes=[pltpu.VMEM((tokens, d), BF16), pltpu.VMEM(w_out.shape, BF16), pltpu.SemaphoreType.DMA],
        compiler_params=pltpu.CompilerParams(vmem_limit_bytes=48 * 2**20),
    )(queries, keys, clusters, w_out)


def on_device(tokens, span_bounds, mention_entity, entity_cluster, entity_table, w_out):
    n, groups = lax.axis_size("mem"), lax.axis_size("dp")
    states, clusters = exchange(
        n, groups, tokens, span_bounds, mention_entity, entity_cluster, entity_table)
    return read_memories(tokens, states.reshape(-1, tokens.shape[1]), clusters, w_out)


def solution(mesh):
    placed = (
        P(("dp", "mem"), None),
        P(None, ("dp", "mem")),
        P(("dp", "mem")),
        P("mem"),
        P("mem", None),
        P(),
    )
    return jax.shard_map(
        on_device, mesh=mesh, in_specs=placed, out_specs=P(("dp", "mem"), None), check_vma=False
    )
```

time: 404 us -> 92.2 us (0.23)
  waiting for transfers between devices: 262 us -> 0 us
  Pallas kernels: 0 us -> 86.2 us
  matrix products: 81.3 us -> 0 us
  other arithmetic: 30.8 us -> 0 us
  between operations: 13.2 us -> 0.02 us
  local copies, waits for them, and re-layouts: 15.8 us -> 5.54 us
    psum x2 -> x0, waiting for transfers between devices: 103 us -> none  [the longest x1 67.4 us: on_device(): lax.psum(partial_groups.astype(jnp.bfloat16), 'mem').astype(jnp.float32)]
    reduce_scatter x1 -> x0, waiting for transfers between devices: 90.9 us -> none  [on_device(): lax.psum_scatter(jnp.dot(picking, mention_vec, preferred_element_type=jnp...]
    pallas_call x0 -> x2, Pallas kernels: none -> 86.2 us  [the longest x1 47.9 us: exchange(): pl.pallas_call(functools.partial(exchange_kernel, n, groups), out_shape=(...]
    dot_general x9 -> x0, matrix products: 81.3 us -> none  [the longest x2 34.1 us: update(): jnp.einsum('htk,khd->thd', probs.astype(jnp.bfloat16), key_rows, preferre...]
    all_gather x1 -> x0, waiting for transfers between devices: 67.8 us -> none  [on_device(): lax.all_gather(entity_state, 'mem', axis=0, tiled=True)]
    reduce_sum x4 -> x0, other arithmetic: 26 us -> none  [the longest x1 22.8 us: update(): totals = totals * rescale + jnp.sum(probs, axis=-1)]
    slice x3 -> x0, local copies, waits for them, and re-layouts: 12.7 us -> none  [on_device(): key_rows = piece_heads[block_start:block_start + block_rows]]
  transfers between devices with their start and end apart: 4 -> 0, of which waited for: 4 -> 0; matrix products, arithmetic and copies ran while one was open for 2% -> 0% of each run, Pallas kernels for 0% -> 0%
where the time goes in v1:
time: 92.2 us; the launch traced here: 91.7 us
  Pallas kernels  86.2 us (93%)
  local copies, waits for them, and re-layouts  5.54 us (6%)
    pallas_call x1, Pallas kernels, exchange(): pl.pallas_call(functools.partial(exchange_kernel, n, groups), out_shape=(...  47.9 us
    pallas_call x1, Pallas kernels, read_memories(): pl.pallas_call(read_kernel, grid=(d // width,), in_specs=[pl.BlockSpec((t...  38.2 us
    unnamed x7, local copies, waits for them, and re-layouts  4.04 us

profile of v1, /device:TPU:0, one launch (start us, length us, event | category | flops | bytes accessed | tf_op | source)
XLA Modules:
  0.0 91.7 jit_solution(3342205259290120757)
XLA Ops:
  0.0 0.8 copy.7
  0.8 0.7 copy.8.ent_col
  1.5 0.8 copy.9.cluster_col
  2.3 0.0 copy-start
  2.3 1.6 %copy-done = bf16[512,2048]{1,0:T(8,128)(2,1)S(1)} copy-done((bf16[512,2048]{1,0:T(8,128)(2,1)S(1)}, bf16[512,2048]{1,0:T(8,128)(2,1)}, u32[]{:S(2)}) %copy-start) | copy-done | bytes 2097176
  3.8 0.0 copy-start.1
  3.9 1.0 %copy-done.1 = bf16[128,2048]{1,0:T(8,128)(2,1)S(1)} copy-done((bf16[128,2048]{1,0:T(8,128)(2,1)S(1)}, bf16[128,2048]{1,0:T(8,128)(2,1)}, u32[]{:S(2)}) %copy-start.1) | copy-done | bytes 524312
  4.9 0.0 copy-start.2
  4.9 0.7 copy-done.2
  5.5 47.9 %shard_map.64 = (bf16[8,4,32,2048]{3,2,1,0:T(8,128)(2,1)}, bf16[64,2048]{1,0:T(8,128)(2,1)S(1)}) custom-call(bf16[512,2048]{1,0:T(8,128)(2,1)S(1)} %copy-done, s32[32,2]{1,0:T(8,128)S(1)} %bitcast.5, s32[32,1]{1,0:T(8,128)S(1)} %copy.8.ent_col, s32[1,32]{1,0:T(1,128)S(1)} %bitcast.7, s32[128,1]{1,0:T(8,128)S(1)} %copy.9.cluster_col, ...), custom_call_target="tpu_custom_call" | custom-call | tf_op jit(solution)/shard_map/pallas_call | solution.py:220
  53.5 38.2 %shard_map.65 = bf16[512,2048]{1,0:T(8,128)(2,1)} custom-call(bf16[512,2048]{1,0:T(8,128)(2,1)S(1)} %copy-done, bf16[1024,2048]{1,0:T(8,128)(2,1)} %bitcast.8, bf16[64,2048]{1,0:T(8,128)(2,1)S(1)} %get-tuple-element.8.c_ref, bf16[2048,2048]{1,0:T(8,128)(2,1)} %w_hbm.1), custom_call_target="tpu_custom_call" | custom-call | tf_op jit(solution)/shard_map/pallas_call | solution.py:278
Async XLA Ops:
  2.3 1.6 %copy-start = (bf16[512,2048]{1,0:T(8,128)(2,1)S(1)}, bf16[512,2048]{1,0:T(8,128)(2,1)}, u32[]{:S(2)}) copy-start(bf16[512,2048]{1,0:T(8,128)(2,1)} %q_ref.1) | copy-start | bytes 6291460
  3.8 1.0 %copy-start.1 = (bf16[128,2048]{1,0:T(8,128)(2,1)S(1)}, bf16[128,2048]{1,0:T(8,128)(2,1)}, u32[]{:S(2)}) copy-start(bf16[128,2048]{1,0:T(8,128)(2,1)} %table.1) | copy-start | bytes 1572868
  4.9 0.7 copy-start.2

commit v2 on v1

v2 whole, which is shorter than its diff:
```python
import functools

import jax
import jax.numpy as jnp
from jax import lax
from jax.experimental import pallas as pl
from jax.experimental.pallas import tpu as pltpu
from jax.sharding import PartitionSpec as P

MESH = pl.DeviceIdType.MESH
HEAD_DIM = 64
CL_SIZE = 16
SLOTS = 4
PIECES = 4
BF16 = jnp.bfloat16
F32 = jnp.float32


def rms_rows(values):
    return values * lax.rsqrt(jnp.mean(values * values, axis=-1, keepdims=True) + 1e-06)


def ring_place(index, depth, width):
    z, y = index // width, index % width
    back = depth - 1 - z
    across = jnp.where(back % 2 == 0, y - 1, width - 1 - y)
    return jnp.where(y == 0, z, depth + back * (width - 1) + across)


def ring_device(place, depth, width):
    rest = jnp.maximum(place - depth, 0)
    back, across = rest // (width - 1), rest % (width - 1)
    y = jnp.where(back % 2 == 0, 1 + across, width - 1 - across)
    return jnp.where(place < depth, place * width, (depth - 1 - back) * width + y)


def fused_kernel(
    n, groups, bounds, ent_row, cluster_row, tokens_hbm, table_hbm, w_hbm,
    out_ref,
    tokens, table, weights, outbox, mentions, states, pooled, clusters, num, den, top, readout,
    load_sem, mem_send, mem_recv, dp_send, dp_recv, pair_send, pair_recv, own_sem,
    ring_send, ring_recv, hand_send, hand_recv,
):
    loads = [
        pltpu.make_async_copy(src, dst, load_sem.at[i])
        for i, (src, dst) in enumerate(((tokens_hbm, tokens), (table_hbm, table), (w_hbm, weights)))
    ]
    for load in loads:
        load.start()
    d = table.shape[1]
    rows = table.shape[0]
    piece = d // PIECES
    depth, width = 4, n // 4
    me, row = lax.axis_index("mem"), lax.axis_index("dp")
    core = row % 2
    sibling = row + 1 - 2 * core
    place = ring_place(me, depth, width)
    right = ring_device((place + 1) % n, depth, width)
    left = ring_device((place + n - 1) % n, depth, width)
    xs = groups // 2

    barrier = pltpu.get_barrier_semaphore()
    for step in range(1, n):
        pl.semaphore_signal(barrier, device_id=(row, (me + step) % n), device_id_type=MESH)
    for step in range(1, xs):
        pl.semaphore_signal(barrier, device_id=((row + 2 * step) % groups, me), device_id_type=MESH)
    pl.semaphore_signal(barrier, device_id=(sibling, me), device_id_type=MESH)

    count = bounds.shape[1]
    length = tokens.shape[0]
    total = n * SLOTS * PIECES
    position = lax.broadcasted_iota(jnp.int32, (length, count), 0)
    covered = ((position >= bounds[0:1, :]) & (position < bounds[1:2, :])).astype(F32).astype(BF16)
    spans = lax.dot_general(
        covered, jnp.ones((length, 128), BF16), (((0,), (0,)), ((), ())), preferred_element_type=F32)
    shard_row = ent_row[...] // rows
    owner = (lax.broadcasted_iota(jnp.int32, (n, count), 0) == shard_row).astype(F32)
    first = lax.broadcasted_iota(jnp.int32, (count, count), 0)
    second = lax.broadcasted_iota(jnp.int32, (count, count), 1)
    before = jnp.dot(
        owner.astype(BF16), (first < second).astype(F32).astype(BF16), preferred_element_type=F32)
    rank = jnp.sum(owner * before, axis=0, keepdims=True).astype(jnp.int32)
    slot_row = shard_row * SLOTS + rank
    loads[0].wait()
    sums = lax.dot_general(covered, tokens[...], (((0,), (0,)), ((), ())), preferred_element_type=F32)
    vectors = (sums / spans[:, 0:1]).astype(BF16)
    line = lax.broadcasted_iota(jnp.int32, (total, count), 0)
    match = slot_row == (line // (SLOTS * PIECES)) * SLOTS + line % SLOTS
    part = (line // SLOTS) % PIECES
    packed = jnp.zeros((total, piece), F32)
    for p in range(PIECES):
        pick = (match & (part == p)).astype(F32).astype(BF16)
        packed += jnp.dot(pick, vectors[:, p * piece:(p + 1) * piece], preferred_element_type=F32)
    local = (ent_row[...] - shard_row * rows + 1).astype(F32)
    ids = jnp.sum(jnp.where(match, local, 0.0), axis=1, keepdims=True) - 1.0
    outbox[:, :, :piece] = packed.astype(BF16).reshape(n, SLOTS * PIECES, piece)
    outbox[:, :, piece:] = jnp.broadcast_to(ids, (total, 128)).astype(BF16).reshape(n, SLOTS * PIECES, 128)

    pl.semaphore_wait(barrier, n - 1 + xs)

    own = pltpu.make_async_copy(outbox.at[me], mentions.at[row, me], own_sem)
    own.start()
    sends = []
    for step in range(1, n):
        to = (me + step) % n
        copy = pltpu.make_async_remote_copy(
            outbox.at[to], mentions.at[row, me], mem_send.at[step], mem_recv.at[step],
            device_id=(row, to), device_id_type=MESH)
        copy.start()
        sends.append(copy)
    own.wait()
    for step in range(1, n):
        src = (me + n - step) % n
        pltpu.make_async_remote_copy(
            outbox.at[src], mentions.at[row, src], mem_send.at[step], mem_recv.at[step],
            device_id=(row, src), device_id_type=MESH).wait_recv()

    def to_replica(block, to, send, recv):
        return pltpu.make_async_remote_copy(
            mentions.at[block], mentions.at[block], send, recv, device_id=(to, me), device_id_type=MESH)

    for step in range(1, xs):
        copy = to_replica(row, (row + 2 * step) % groups, dp_send.at[step], dp_recv.at[step])
        copy.start()
        sends.append(copy)
    copy = to_replica(row, sibling, pair_send.at[0], pair_recv.at[0])
    copy.start()
    sends.append(copy)
    for step in range(1, xs):
        src = (row + groups - 2 * step) % groups
        to_replica(src, src, dp_send.at[step], dp_recv.at[step]).wait_recv()
        copy = to_replica(src, sibling, pair_send.at[step], pair_recv.at[step])
        copy.start()
        sends.append(copy)
    for step in range(xs):
        src = (sibling + groups - 2 * step) % groups
        to_replica(src, sibling, pair_send.at[step], pair_recv.at[step]).wait_recv()

    loads[1].wait()
    arrived = groups * n * SLOTS * PIECES
    box = mentions[...].reshape(arrived, piece + 128)
    line = lax.broadcasted_iota(jnp.int32, (arrived, rows), 0)
    entity = lax.broadcasted_iota(jnp.int32, (arrived, rows), 1).astype(F32)
    named = box[:, piece:].astype(F32) == entity
    part = (line // SLOTS) % PIECES
    square = jnp.zeros((rows, 1), F32)
    for p in range(PIECES):
        pick = (named & (part == p)).astype(F32).astype(BF16)
        got = lax.dot_general(pick, box[:, :piece], (((0,), (0,)), ((), ())), preferred_element_type=F32)
        got += table[:, p * piece:(p + 1) * piece].astype(F32)
        pooled[:, p * piece:(p + 1) * piece] = got
        square += jnp.sum(got * got, axis=-1, keepdims=True)
    state = (pooled[...] * lax.rsqrt(square / d + 1e-06)).astype(BF16)
    quarter = rows // 4
    states[0, :, :, :d] = state.reshape(4, quarter, d)
    kind = lax.broadcasted_iota(jnp.int32, (128, rows), 0)
    group = (cluster_row[...] == kind).astype(F32).T.astype(BF16)
    states[0, :, :, d:] = group.reshape(4, quarter, 128)

    half = n // 2

    def portion(way, step):
        if step < half:
            return pl.ds(2 * core, 2)
        return pl.ds(2 * core + way, 1)

    def ring_copy(way, step):
        src = step - 1 if way == 0 else (n - step + 1) % n
        dst = step if way == 0 else n - step
        quarters = portion(way, step)
        return pltpu.make_async_remote_copy(
            states.at[src, quarters], states.at[dst, quarters], ring_send.at[way, step], ring_recv.at[way, step],
            device_id=(row, right if way == 0 else left), device_id_type=MESH)

    def hand_copy(way, step, to_core):
        dst = step if way == 0 else n - step
        if step < half:
            quarters = pl.ds(2 * to_core, 2)
        else:
            quarters = pl.ds(2 * to_core + way, 1)
        return pltpu.make_async_remote_copy(
            states.at[dst, quarters], states.at[dst, quarters], hand_send.at[way, step], hand_recv.at[way, step],
            device_id=(sibling, me), device_id_type=MESH)

    def serve(step):
        for way in range(2):
            ring_copy(way, step).wait_recv()
            if step < half:
                copy = ring_copy(way, step + 1)
                copy.start()
                sends.append(copy)
            copy = hand_copy(way, step, core)
            copy.start()
            sends.append(copy)

    for way in range(2):
        copy = ring_copy(way, 1)
        copy.start()
        sends.append(copy)

    width = 2 * HEAD_DIM
    low = lax.broadcasted_iota(jnp.int32, (1, width), 1) < HEAD_DIM
    one, zero = jnp.ones((), BF16), jnp.zeros((), BF16)

    def lanes_of(index, size):
        return pl.ds(pl.multiple_of(index * size, size), size)

    def read_part(lanes, slots):
        q = tokens[:, lanes] * BF16(HEAD_DIM ** -0.5)
        keys = jnp.concatenate([states[slot, :, :, lanes].reshape(rows, width) for slot in slots], axis=0)
        sides, tops = [], []
        for h in range(2):
            mine = low if h == 0 else jnp.logical_not(low)
            scores = lax.dot_general(
                jnp.where(mine, q, zero), keys, (((1,), (1,)), ((), ())), preferred_element_type=F32)
            most = jnp.max(scores, axis=-1, keepdims=True)
            probs = jnp.exp(scores - most).astype(BF16)
            sides.append(jnp.dot(probs, jnp.where(mine, keys, one), preferred_element_type=F32))
            tops.append(most)
        return (
            jnp.where(low, sides[0], sides[1]),
            pltpu.roll(jnp.where(low, sides[1], sides[0]), HEAD_DIM, 1),
            jnp.where(low, tops[0], tops[1]),
        )

    def merge(lanes, part):
        new_num, new_den, new_top = part
        old_top = top[:, lanes]
        both = jnp.maximum(old_top, new_top)
        keep, add = jnp.exp(old_top - both), jnp.exp(new_top - both)
        return num[:, lanes] * keep + new_num * add, den[:, lanes] * keep + new_den * add, both

    def attend(slots, start, stop):
        @pl.loop(start, stop)
        def _(pair):
            lanes = lanes_of(pair, width)
            part = read_part(lanes, slots)
            if 0 not in slots:
                part = merge(lanes, part)
            num[:, lanes], den[:, lanes], top[:, lanes] = part

    pairs = d // width
    for step in range(half - 1):
        slots = [0] if step == 0 else [step, n - step]
        split = pairs // 2 if step == half - 2 else 3 * pairs // 4
        attend(slots, 0, split)
        serve(step + 1)
        attend(slots, split, pairs)
        if step == half - 2:
            serve(half)
            for way in range(2):
                hand_copy(way, half, 1 - core).wait_recv()
        for way in range(2):
            hand_copy(way, step + 1, 1 - core).wait_recv()

    kinds = clusters.shape[0]
    every = states[...].reshape(n * rows, d + 128)
    grouped = lax.dot_general(every[:, d:], every[:, :d], (((0,), (0,)), ((), ())), preferred_element_type=F32)
    clusters[...] = rms_rows(grouped[:kinds]).astype(BF16)

    heads = 256 // kinds
    wide = heads * HEAD_DIM
    head_of = lax.broadcasted_iota(jnp.int32, (1, wide), 1) // HEAD_DIM

    @pl.loop(0, d // wide)
    def _(index):
        lanes = lanes_of(index, wide)
        q = tokens[:, lanes] * BF16(HEAD_DIM ** -0.5)
        mem = clusters[:, lanes]
        keys = jnp.concatenate([jnp.where(head_of == h, mem, zero) for h in range(heads)], axis=0)
        ones = jnp.concatenate(
            [jnp.broadcast_to(jnp.where(head_of == h, one, zero), (kinds, wide)) for h in range(heads)], axis=0)
        scores = lax.dot_general(q, keys, (((1,), (1,)), ((), ())), preferred_element_type=F32)
        column = lax.broadcasted_iota(jnp.int32, (1, heads * kinds), 1) // kinds
        shift = jnp.zeros_like(scores)
        for h in range(heads):
            most = jnp.max(jnp.where(column == h, scores, -jnp.inf), axis=-1, keepdims=True)
            shift = jnp.where(column == h, most, shift)
        probs = jnp.exp(scores - shift).astype(BF16)
        read = jnp.dot(probs, keys, preferred_element_type=F32) / jnp.dot(
            probs, ones, preferred_element_type=F32)
        for inner in range(wide // width):
            part_lanes = lanes_of(index * (wide // width) + inner, width)
            new_num, new_den, _ = merge(part_lanes, read_part(part_lanes, [half - 1, half + 1, half]))
            read_here = new_num / new_den + read[:, inner * width:(inner + 1) * width]
            readout[:, part_lanes] = read_here.astype(BF16)

    loads[2].wait()
    out_ref[...] = rms_rows(
        jnp.dot(readout[...], weights[...], preferred_element_type=F32)).astype(BF16)
    for copy in sends:
        copy.wait_send()


def on_device(tokens, span_bounds, mention_entity, entity_cluster, entity_table, w_out):
    n, groups = lax.axis_size("mem"), lax.axis_size("dp")
    rows, d = entity_table.shape
    count = mention_entity.shape[0]
    kinds = rows * n // CL_SIZE
    piece = d // PIECES
    vmem, anywhere = pl.BlockSpec(memory_space=pltpu.VMEM), pl.BlockSpec(memory_space=pl.ANY)
    dma = pltpu.SemaphoreType.DMA
    full = tokens.shape
    return pl.pallas_call(
        functools.partial(fused_kernel, n, groups),
        out_shape=jax.ShapeDtypeStruct(full, BF16),
        in_specs=[vmem] * 3 + [anywhere] * 3,
        out_specs=vmem,
        scratch_shapes=[
            pltpu.VMEM(full, BF16),
            pltpu.VMEM((rows, d), BF16),
            pltpu.VMEM(w_out.shape, BF16),
            pltpu.VMEM((n, SLOTS * PIECES, piece + 128), BF16),
            pltpu.VMEM((groups, n, SLOTS * PIECES, piece + 128), BF16),
            pltpu.VMEM((n, 4, rows // 4, d + 128), BF16),
            pltpu.VMEM((rows, d), F32),
            pltpu.VMEM((kinds, d), BF16),
            pltpu.VMEM(full, F32), pltpu.VMEM(full, F32), pltpu.VMEM(full, F32),
            pltpu.VMEM(full, BF16),
            dma((3,)),
            dma((n,)), dma((n,)), dma((groups,)), dma((groups,)), dma((groups,)), dma((groups,)), dma,
            dma((2, n)), dma((2, n)), dma((2, n)), dma((2, n)),
        ],
        compiler_params=pltpu.CompilerParams(
            collective_id=0, has_side_effects=True, vmem_limit_bytes=58 * 2**20),
    )(span_bounds, mention_entity.reshape(1, count), entity_cluster.reshape(1, rows), tokens, entity_table, w_out)


def solution(mesh):
    placed = (
        P(("dp", "mem"), None),
        P(None, ("dp", "mem")),
        P(("dp", "mem")),
        P("mem"),
        P("mem", None),
        P(),
    )
    return jax.shard_map(
        on_device, mesh=mesh, in_specs=placed, out_specs=P(("dp", "mem"), None), check_vma=False
    )
```

time: 92.2 us -> 85.4 us (0.926)
  Pallas kernels: 86.2 us -> 82 us
  local copies, waits for them, and re-layouts: 5.54 us -> 3.16 us
    pallas_call x2 -> x1, Pallas kernels: 86.2 us -> 82 us  [on_device(): pl.pallas_call(functools.partial(fused_kernel, n, groups), out_shape=jax....]
    reshape x2 -> x0, local copies, waits for them, and re-layouts: 1.5 us -> none  [the longest x1 0.76 us: exchange(): entity_cluster.reshape(rows, 1)]
    unnamed x7 -> x1, local copies, waits for them, and re-layouts: 4.04 us -> 3.16 us
where the time goes in v2:
time: 85.4 us; the launch traced here: 85.2 us
  Pallas kernels  82 us (96%)
  local copies, waits for them, and re-layouts  3.16 us (4%)
    pallas_call x1, Pallas kernels, on_device(): pl.pallas_call(functools.partial(fused_kernel, n, groups), out_shape=jax....  82 us
    unnamed x1, local copies, waits for them, and re-layouts  3.16 us

profile of v2, /device:TPU:0, one launch (start us, length us, event | category | flops | bytes accessed | tf_op | source)
XLA Modules:
  0.0 85.2 jit_solution(1951902171403163926)
XLA Ops:
  0.0 82.0 %shard_map.64 = bf16[512,2048]{1,0:T(8,128)(2,1)} custom-call(s32[2,32]{1,0:T(2,128)} %bounds.1, s32[1,32]{1,0:T(1,128)} %bitcast.2, s32[1,128]{1,0:T(1,128)} %bitcast.3, bf16[512,2048]{1,0:T(8,128)(2,1)} %tokens_hbm.1, bf16[128,2048]{1,0:T(8,128)(2,1)} %table_hbm.1, bf16[2048,2048]{1,0:T(8,128)(2,1)} %w_hbm.1), custom_call_target="tpu_custom_call" | custom-call | tf_op jit(solution)/shard_map/pallas_call | solution.py:304
  82.0 3.2 %copy.8 = bf16[512,2048]{1,0:T(8,128)(2,1)} copy(bf16[512,2048]{1,0:T(8,128)(2,1)} %shard_map.64) | data formatting | bytes 4194304

commit v3 on v2

--- a/solution.py
+++ b/solution.py
@@ -231,7 +231,7 @@
         return num[:, lanes] * keep + new_num * add, den[:, lanes] * keep + new_den * add, both
 
     def attend(slots, start, stop):
-        @pl.loop(start, stop)
+        @pl.loop(start, stop, unroll=4 if slots == [0] else 2)
         def _(pair):
             lanes = lanes_of(pair, width)
             part = read_part(lanes, slots)
@@ -240,18 +240,25 @@
             num[:, lanes], den[:, lanes], top[:, lanes] = part
 
     pairs = d // width
-    for step in range(half - 1):
-        slots = [0] if step == 0 else [step, n - step]
-        split = pairs // 2 if step == half - 2 else 3 * pairs // 4
-        attend(slots, 0, split)
-        serve(step + 1)
-        attend(slots, split, pairs)
-        if step == half - 2:
-            serve(half)
-            for way in range(2):
-                hand_copy(way, half, 1 - core).wait_recv()
+    attend([0], 0, 3 * pairs // 4)
+    serve(1)
+    attend([0], 3 * pairs // 4, pairs)
+    early = []
+    for step in range(1, half - 1):
+        if step > 1:
+            serve(step)
+        early += [step, n - step]
+    for step in range(1, half - 1):
         for way in range(2):
-            hand_copy(way, step + 1, 1 - core).wait_recv()
+            hand_copy(way, step, 1 - core).wait_recv()
+    attend(early, 0, pairs // 2)
+    serve(half - 1)
+    attend(early, pairs // 2, 7 * pairs // 8)
+    serve(half)
+    attend(early, 7 * pairs // 8, pairs)
+    for step in range(half - 1, half + 1):
+        for way in range(2):
+            hand_copy(way, step, 1 - core).wait_recv()
 
     kinds = clusters.shape[0]
     every = states[...].reshape(n * rows, d + 128)

time: 85.4 us -> 81.4 us (0.953)
  Pallas kernels: 82 us -> 78.1 us
    pallas_call x1, Pallas kernels: 82 us -> 78.1 us  [on_device(): pl.pallas_call(functools.partial(fused_kernel, n, groups), out_shape=jax....]
where the time goes in v3:
time: 81.4 us; the launch traced here: 81.3 us
  Pallas kernels  78.1 us (96%)
  local copies, waits for them, and re-layouts  3.16 us (4%)
    pallas_call x1, Pallas kernels, on_device(): pl.pallas_call(functools.partial(fused_kernel, n, groups), out_shape=jax....  78.1 us
    unnamed x1, local copies, waits for them, and re-layouts  3.16 us

profile of v3, /device:TPU:0, one launch (start us, length us, event | category | flops | bytes accessed | tf_op | source)
XLA Modules:
  0.0 81.3 jit_solution(11105261128107621427)
XLA Ops:
  0.0 78.1 %shard_map.64 = bf16[512,2048]{1,0:T(8,128)(2,1)} custom-call(s32[2,32]{1,0:T(2,128)} %bounds.1, s32[1,32]{1,0:T(1,128)} %bitcast.2, s32[1,128]{1,0:T(1,128)} %bitcast.3, bf16[512,2048]{1,0:T(8,128)(2,1)} %tokens_hbm.1, bf16[128,2048]{1,0:T(8,128)(2,1)} %table_hbm.1, bf16[2048,2048]{1,0:T(8,128)(2,1)} %w_hbm.1), custom_call_target="tpu_custom_call" | custom-call | tf_op jit(solution)/shard_map/pallas_call | solution.py:311
  78.1 3.2 %copy.8 = bf16[512,2048]{1,0:T(8,128)(2,1)} copy(bf16[512,2048]{1,0:T(8,128)(2,1)} %shard_map.64) | data formatting | bytes 4194304

commit v4 on v3

--- a/solution.py
+++ b/solution.py
@@ -186,17 +186,11 @@
         for way in range(2):
             ring_copy(way, step).wait_recv()
             if step < half:
-                copy = ring_copy(way, step + 1)
-                copy.start()
-                sends.append(copy)
-            copy = hand_copy(way, step, core)
-            copy.start()
-            sends.append(copy)
+                ring_copy(way, step + 1).start()
+            hand_copy(way, step, core).start()
 
     for way in range(2):
-        copy = ring_copy(way, 1)
-        copy.start()
-        sends.append(copy)
+        ring_copy(way, 1).start()
 
     width = 2 * HEAD_DIM
     low = lax.broadcasted_iota(jnp.int32, (1, width), 1) < HEAD_DIM
@@ -230,19 +224,22 @@
         keep, add = jnp.exp(old_top - both), jnp.exp(new_top - both)
         return num[:, lanes] * keep + new_num * add, den[:, lanes] * keep + new_den * add, both
 
-    def attend(slots, start, stop):
-        @pl.loop(start, stop, unroll=4 if slots == [0] else 2)
-        def _(pair):
-            lanes = lanes_of(pair, width)
-            part = read_part(lanes, slots)
-            if 0 not in slots:
-                part = merge(lanes, part)
-            num[:, lanes], den[:, lanes], top[:, lanes] = part
+    def attend(slots, group, served):
+        @pl.loop(0, d // width // group)
+        def _(index):
+            for inner in range(group):
+                lanes = lanes_of(index * group + inner, width)
+                part = read_part(lanes, slots)
+                if 0 not in slots:
+                    part = merge(lanes, part)
+                num[:, lanes], den[:, lanes], top[:, lanes] = part
+            for last, step in served:
+                @pl.when(index == last)
+                def _():
+                    serve(step)
 
     pairs = d // width
-    attend([0], 0, 3 * pairs // 4)
-    serve(1)
-    attend([0], 3 * pairs // 4, pairs)
+    attend([0], 4, [(pairs // 4 - 2, 1)])
     early = []
     for step in range(1, half - 1):
         if step > 1:
@@ -251,11 +248,7 @@
     for step in range(1, half - 1):
         for way in range(2):
             hand_copy(way, step, 1 - core).wait_recv()
-    attend(early, 0, pairs // 2)
-    serve(half - 1)
-    attend(early, pairs // 2, 7 * pairs // 8)
-    serve(half)
-    attend(early, 7 * pairs // 8, pairs)
+    attend(early, 2, [(pairs // 4 - 1, half - 1), (pairs // 2 - 2, half)])
     for step in range(half - 1, half + 1):
         for way in range(2):
             hand_copy(way, step, 1 - core).wait_recv()
@@ -297,6 +290,10 @@
         jnp.dot(readout[...], weights[...], preferred_element_type=F32)).astype(BF16)
     for copy in sends:
         copy.wait_send()
+    for step in range(1, half + 1):
+        for way in range(2):
+            ring_copy(way, step).wait_send()
+            hand_copy(way, step, core).wait_send()
 
 
 def on_device(tokens, span_bounds, mention_entity, entity_cluster, entity_table, w_out):

time: 81.4 us -> 81.6 us (level)
  no operation moved by 1% of the time
where the time goes in v4:
time: 81.6 us; the launch traced here: 81.5 us
  Pallas kernels  78.3 us (96%)
  local copies, waits for them, and re-layouts  3.16 us (4%)
    pallas_call x1, Pallas kernels, on_device(): pl.pallas_call(functools.partial(fused_kernel, n, groups), out_shape=jax....  78.3 us
    unnamed x1, local copies, waits for them, and re-layouts  3.16 us

profile of v4, /device:TPU:0, one launch (start us, length us, event | category | flops | bytes accessed | tf_op | source)
XLA Modules:
  0.0 81.5 jit_solution(9319697828012045540)
XLA Ops:
  0.0 78.3 %shard_map.64 = bf16[512,2048]{1,0:T(8,128)(2,1)} custom-call(s32[2,32]{1,0:T(2,128)} %bounds.1, s32[1,32]{1,0:T(1,128)} %bitcast.2, s32[1,128]{1,0:T(1,128)} %bitcast.3, bf16[512,2048]{1,0:T(8,128)(2,1)} %tokens_hbm.1, bf16[128,2048]{1,0:T(8,128)(2,1)} %table_hbm.1, bf16[2048,2048]{1,0:T(8,128)(2,1)} %w_hbm.1), custom_call_target="tpu_custom_call" | custom-call | tf_op jit(solution)/shard_map/pallas_call | solution.py:308
  78.3 3.2 %copy.8 = bf16[512,2048]{1,0:T(8,128)(2,1)} copy(bf16[512,2048]{1,0:T(8,128)(2,1)} %shard_map.64) | data formatting | bytes 4194304
